TPU v7x, 256 devices: a whole 4x4x8 slice. The times are simulated.
256 devices in a mesh: view: 8 (over x, core), band: 32 (over z, y).
Axes of the slice: x: 4, y: 4, z: 8, core: 2. Of those that a mesh axis runs over, the one named last changes fastest.
Arguments:
- latents: bfloat16 [8, 8192, 1024], P('view', 'band'), may hold values from -170 to 170
- w_qkv: bfloat16 [1024, 3072], replicated, may hold values from -0.75 to 0.75
- w_out: bfloat16 [1024, 1024], replicated, may hold values from -0.1875 to 0.1875
- epipolar_bands: int32 [8, 32, 8], replicated, may hold values from -1 to 31, as said below
- object_token_mask: int32 [8, 8192], replicated, may hold values from 0 to 1, as said below
Outputs:
- updated: float32 [8, 8192, 1024], P('view', 'band')
Inputs may be any that keep to these rules, and one draw needn't show every extreme that they name: epipolar_bands[v, b, w] is -1 where w is v or the epipolar lines miss view w; otherwise a band of view w within 2 bands of b. For every query band and every nonzero distance d, at most 2 views have band b + d listed, and some query band lists 2 views at one such distance. `object_token_mask`: the first token of every band is 1.
All inputs are finite; a program needn't handle non-finite values.
Results may differ from a plain program's by a relative error of at most 0.023.
Values may be sent and summed in bfloat16 or wider, within the bound.
A program may use at most 128 MiB of HBM per device.

v0:
```python
import jax
import jax.numpy as jnp
from jax import lax
from jax.sharding import PartitionSpec as P

HEADS = 16
HEAD_DIM = 64
REACH = 2
MOST = 2


def with_halo(cells, sides, width):
    for axis, dim in sides:
        count = lax.axis_size(axis)
        ends = count - 1
        head = lax.slice_in_dim(cells, 0, width, axis=dim)
        tail = lax.slice_in_dim(cells, cells.shape[dim] - width, cells.shape[dim], axis=dim)
        cells = jnp.concatenate(
            [
                lax.ppermute(tail, axis, [(i, (i + 1) % count) for i in range(ends)]),
                cells,
                lax.ppermute(head, axis, [((i + 1) % count, i) for i in range(ends)]),
            ],
            axis=dim,
        )
    return cells


def from_behind(block, axis, distance):
    devices = range(lax.axis_size(axis))
    route = [(i - distance, i) for i in devices if i - distance in devices]
    return lax.ppermute(block, axis, route)


def attend_heads(queries, key_rows, values, usable):
    count_of_rows = queries.shape[0]
    key_count = key_rows.shape[0]
    groups = HEADS // 4
    score_scale = HEAD_DIM ** (-0.5)
    query_parts = queries.reshape(count_of_rows, groups, 4, HEAD_DIM).transpose(1, 0, 2, 3)
    key_parts = key_rows.reshape(key_count, groups, 4, HEAD_DIM).transpose(1, 0, 2, 3)
    value_parts = values.reshape(key_count, groups, 4, HEAD_DIM).transpose(1, 0, 2, 3)

    def per_group(operands):
        query_block, key_block, value_block = operands
        scores = (
            jnp.einsum("qhd,khd->hqk", query_block, key_block, preferred_element_type=jnp.float32)
            * score_scale
        )
        scores = jnp.where(usable[None, None, :], scores, -1e30)
        row_top = jnp.max(scores, axis=-1, keepdims=True)
        raised = jnp.exp(scores - row_top)
        attention = (raised / jnp.sum(raised, axis=-1, keepdims=True)).astype(jnp.bfloat16)
        return jnp.einsum(
            "hqk,khd->qhd", attention, value_block, preferred_element_type=jnp.float32
        )

    blended = lax.map(per_group, (query_parts, key_parts, value_parts))
    return (
        blended.transpose(1, 0, 2, 3).reshape(count_of_rows, HEADS * HEAD_DIM).astype(jnp.bfloat16)
    )


def offset_payload(offset, pick_from, epipolar_bands, local_view, my_band, band_list):
    slot_ids = jnp.arange(MOST, dtype=jnp.int32)
    requester = my_band - offset
    inside = (requester >= 0) & (requester < band_list)
    wanted = epipolar_bands[local_view, jnp.clip(requester, 0, band_list - 1)]
    matches = (wanted == my_band) & inside
    match_count = matches.astype(jnp.int32)
    ranks = jnp.cumsum(match_count) - match_count
    picker = (matches[None, :] & (ranks[None, :] == slot_ids[:, None])).astype(jnp.bfloat16)
    return jnp.einsum("rw,wtc->rtc", picker, pick_from, preferred_element_type=jnp.float32).astype(
        jnp.bfloat16
    )


def locate_slabs(stacked, local_list, my_band, view_list):
    view_numbers = jnp.arange(view_list, dtype=jnp.int32)
    distance = local_list - my_band
    present = local_list >= 0
    same_shift = (
        (distance[:, None] == distance[None, :])
        & present[None, :]
        & (view_numbers[None, :] < view_numbers[:, None])
    )
    my_ranks = jnp.sum(same_shift.astype(jnp.int32), axis=1)
    position = jnp.where(distance < 0, distance + REACH, distance + REACH - 1)
    location = jnp.where(distance == 0, view_numbers, view_list + position * MOST + my_ranks)
    location = jnp.where(present, location, 0)
    return jnp.take(stacked, location, axis=0)


def body(latents, w_qkv, w_out, epipolar_bands, object_token_mask):
    view_list = lax.axis_size("view")
    band_list = lax.axis_size("band")
    local_view = lax.axis_index("view")
    my_band = lax.axis_index("band")
    count_of_rows = latents.shape[1]
    width = latents.shape[2]
    tokens = latents[0]
    projected = jnp.dot(tokens, w_qkv, preferred_element_type=jnp.float32).astype(jnp.bfloat16)
    queries = projected[:, :width]
    key_value = projected[:, width:]
    active_flags = object_token_mask.reshape(view_list, band_list, count_of_rows) > 0
    local_list = epipolar_bands[local_view, my_band]
    view_numbers = jnp.arange(view_list, dtype=jnp.int32)
    nonzero = [distance_step for distance_step in range(-REACH, REACH + 1) if distance_step != 0]
    nearby = with_halo(key_value[None], (("band", 0),), 1)
    gathered = lax.all_gather(key_value[None], "view", axis=0, tiled=True)
    sources = [gathered]
    for offset in nonzero:
        payload = offset_payload(offset, gathered, epipolar_bands, local_view, my_band, band_list)
        sources.append(from_behind(payload, "band", -offset))
    epipolar = locate_slabs(jnp.concatenate(sources, axis=0), local_list, my_band, view_list)
    slabs = jnp.concatenate([nearby, epipolar], axis=0)
    neighbour_index = my_band + jnp.arange(-1, 2, dtype=jnp.int32)
    neighbour_inside = (neighbour_index >= 0) & (neighbour_index < band_list)
    neighbour_active = (
        active_flags[local_view, jnp.clip(neighbour_index, 0, band_list - 1)]
        & neighbour_inside[:, None]
    )
    far_live = (
        active_flags[view_numbers, jnp.clip(local_list, 0, band_list - 1)]
        & (local_list >= 0)[:, None]
        & (view_numbers != local_view)[:, None]
    )
    usable = jnp.concatenate([neighbour_active, far_live], axis=0).reshape(-1)
    flattened = slabs.reshape(-1, 2 * width)
    blended = attend_heads(queries, flattened[:, :width], flattened[:, width:], usable)
    updated = tokens.astype(jnp.float32) + jnp.dot(
        blended, w_out, preferred_element_type=jnp.float32
    )
    return updated[None]


def solution(mesh):
    placed = (P("view", "band", None), P(), P(), P(), P())
    return jax.shard_map(
        body, mesh=mesh, in_specs=placed, out_specs=P("view", "band", None), check_vma=False
    )
```

profile of v0, /device:TPU:1, one launch (start us, length us, event | category | flops | bytes accessed | tf_op | source)
XLA Modules:
  0.0 399.5 jit_solution(18044199207738665563)
XLA Ops:
  6.5 0.0 copy-start
  6.5 0.0 all-gather.3.cloned.1.call-start
  6.5 4.9 %convolution_convert_fusion = bf16[256,3072]{1,0:T(8,128)(2,1)S(1)} fusion(bf16[1024,3072]{1,0:T(8,128)(2,1)} %param.8, bf16[1,256,1024]{2,1,0:T(8,128)(2,1)} %param.7), kind=kOutput, calls=%fused_computation.41 | convolution fusion | flops 1611399168 | bytes 8388608 | tf_op jit(solution)/shard_map/dot_general | solution.py:102
  11.4 0.0 copy-start.2
  11.5 1.1 copy-done.2
  12.6 1.2 slice_bitcast_fusion
  13.8 0.0 all-gather.3.cloned.1.call-update
  13.8 1.3 collective-permute-start.1
  15.2 1.9 slice.24
  17.1 0.0 copy-done.6
  17.1 0.3 clamp_reduce_fusion
  17.4 0.1 reduce.4
  17.5 0.1 reduce.2
  17.6 0.1 reduce.8
  17.8 0.1 reduce.6
  17.9 0.2 reduce-window.33
  18.1 0.2 reduce-window.32
  18.2 0.2 reduce-window.35
  18.4 0.2 reduce-window.34
  18.7 0.6 gather_fusion.1
  19.3 0.2 compare_reduce_fusion
  19.5 0.2 convert_reduce_fusion.4
  19.7 0.6 gather_fusion.2
  20.3 0.1 broadcast_and_fusion
  20.4 0.1 and_and_fusion
  20.5 2.0 copy.37
  22.6 47.9 %all-gather.3.cloned.1.call-done = bf16[2048,2048]{1,0:T(8,128)(2,1)} async-done(((bf16[256,2048]{1,0:T(8,128)(2,1)}), bf16[2048,2048]{1,0:T(8,128)(2,1)}) %all-gather.3.cloned.1.call-update) | async-done | bytes 8388624 | tf_op jit(solution)/shard_map/all_gather | solution.py:110
  70.5 10.9 %fusion.50 = bf16[2,256,2048]{2,0,1:T(2,128)(2,1)} fusion(bf16[8,256,2048]{2,1,0:T(8,128)(2,1)} %bitcast.134, pred[8]{0:T(512)(128)(4,1)S(1)} %reduce.2, s32[8]{0:T(128)S(1)} %bitcast_subtract_fusion.3), kind=kOutput, calls=%fused_computation.42 | convolution fusion | flops 17825824 | bytes 10485800 | tf_op jit(solution)/shard_map/rw,wtc->rtc/dot_general | solution.py:73
  81.4 6.0 %collective-permute-start.2 = (bf16[2,256,2048]{2,0,1:T(2,128)(2,1)}, bf16[2,256,2048]{2,0,1:T(2,128)(2,1)}, u32[]{:S(2)}, u32[]{:S(2)}) collective-permute-start(bf16[2,256,2048]{2,0,1:T(2,128)(2,1)} %fusion.50), channel_id=1, source_target_pairs={{0,2},{1,3},{2,4},{3,5},{4,6},{5,7},{6,8},{7,9},{8,10},{9,11},{10,... | collective-permute-start | bytes 6291464 | tf_op jit(solution)/shard_map/ppermute | solution.py:32
  87.4 0.0 copy-done.1
  87.4 7.0 %fusion.53 = bf16[2,256,2048]{2,0,1:T(2,128)(2,1)} fusion(bf16[8,256,2048]{2,1,0:T(8,128)(2,1)S(1)} %bitcast.136, pred[8]{0:T(512)(128)(4,1)S(1)} %reduce.4, s32[8]{0:T(128)S(1)} %bitcast_subtract_fusion.2), kind=kOutput, calls=%fused_computation.43 | convolution fusion | flops 17825824 | bytes 10485800 | tf_op jit(solution)/shard_map/rw,wtc->rtc/dot_general | solution.py:73
  94.4 3.5 collective-permute-start.3
  97.9 7.0 %fusion.56 = bf16[2,256,2048]{2,0,1:T(2,128)(2,1)} fusion(bf16[8,256,2048]{2,1,0:T(8,128)(2,1)S(1)} %bitcast.137, pred[8]{0:T(512)(128)(4,1)S(1)} %reduce.6, s32[8]{0:T(128)S(1)} %bitcast_subtract_fusion.1), kind=kOutput, calls=%fused_computation.44 | convolution fusion | flops 17825824 | bytes 10485800 | tf_op jit(solution)/shard_map/rw,wtc->rtc/dot_general | solution.py:73
  104.9 1.3 collective-permute-start.4
  106.2 7.0 %fusion.59 = bf16[2,256,2048]{2,0,1:T(2,128)(2,1)} fusion(bf16[8,256,2048]{2,1,0:T(8,128)(2,1)S(1)} %bitcast.138, pred[8]{0:T(512)(128)(4,1)S(1)} %reduce.8, s32[8]{0:T(128)S(1)} %bitcast_subtract_fusion), kind=kOutput, calls=%fused_computation.45 | convolution fusion | flops 17825824 | bytes 10485800 | tf_op jit(solution)/shard_map/rw,wtc->rtc/dot_general | solution.py:73
  113.2 1.3 collective-permute-start.5
  114.5 8.3 %constant_dynamic-update-slice_fusion = bf16[16,256,2048]{2,1,0:T(8,128)(2,1)} fusion(bf16[8,256,2048]{2,1,0:T(8,128)(2,1)} %bitcast.135), kind=kLoop, calls=%fused_computation.56 | loop fusion | bytes 16777216
  122.8 8.4 %collective-permute-done.2 = bf16[2,256,2048]{2,0,1:T(2,128)(2,1)} collective-permute-done((bf16[2,256,2048]{2,0,1:T(2,128)(2,1)}, bf16[2,256,2048]{2,0,1:T(2,128)(2,1)}, u32[]{:S(2)}, u32[]{:S(2)}) %collective-permute-start.2) | collective-permute-done | bytes 2097184 | tf_op jit(solution)/shard_map/ppermute | solution.py:32
  131.2 93.0 %collective-permute-start = (bf16[1,256,2048]{2,1,0:T(8,128)(2,1)S(1)}, bf16[1,256,2048]{2,1,0:T(8,128)(2,1)}, u32[]{:S(2)}, u32[]{:S(2)}) collective-permute-start(bf16[1,256,2048]{2,1,0:T(8,128)(2,1)S(1)} %get-tuple-element.67), channel_id=1, source_target_pairs={{0,1},{1,2},{2,3},{3,4},{4,5},{5,6},{6,7},{7,8},{8,9},{9,10},{10,1... | collective-permute-start | bytes 3145736 | tf_op jit(solution)/shard_map/ppermute | solution.py:20
  224.1 3.9 copy_dynamic-update-slice_fusion.3
  228.0 0.0 collective-permute-done.3
  228.0 3.8 copy_dynamic-update-slice_fusion.2
  231.8 35.2 %collective-permute-done.4 = bf16[2,256,2048]{2,0,1:T(2,128)(2,1)} collective-permute-done((bf16[2,256,2048]{2,0,1:T(2,128)(2,1)}, bf16[2,256,2048]{2,0,1:T(2,128)(2,1)}, u32[]{:S(2)}, u32[]{:S(2)}) %collective-permute-start.4) | collective-permute-done | bytes 2097184 | tf_op jit(solution)/shard_map/ppermute | solution.py:32
  266.9 3.8 copy_dynamic-update-slice_fusion.1
  270.8 0.0 collective-permute-done.5
  270.8 2.2 copy_dynamic-update-slice_fusion
  273.0 10.4 %gather_fusion = bf16[8,256,2048]{2,1,0:T(8,128)(2,1)} fusion(bf16[16,256,2048]{2,1,0:T(8,128)(2,1)} %copy_dynamic-update-slice_fusion, s32[1024]{0:T(1024)S(1)} %pad_clamp_fusion), kind=kCustom, calls=%fused_computation | custom fusion | bytes 16777248 | tf_op jit(solution)/shard_map/jit(_take)/gather | solution.py:91
  283.4 7.5 %broadcast_select_fusion = bf16[8,256,2048]{2,1,0:T(8,128)(2,1)} fusion(bf16[8,256,2048]{2,1,0:T(8,128)(2,1)} %gather_fusion, pred[8]{0:T(512)(128)(4,1)S(1)} %compare_and_fusion.1), kind=kLoop, calls=%fused_computation.32 | loop fusion | flops 4194304 | bytes 16777224 | tf_op jit(solution)/shard_map/jit(_take)/select_n | solution.py:91
  290.8 0.0 collective-permute-done.1
  290.8 0.0 collective-permute-done
  290.8 9.5 %pad_maximum_fusion = bf16[11,256,2048]{2,1,0:T(8,128)(2,1)} fusion(bf16[8,256,2048]{2,1,0:T(8,128)(2,1)} %broadcast_select_fusion, bf16[1,256,2048]{2,1,0:T(8,128)(2,1)} %collective-permute-done.1, bf16[1,256,2048]{2,1,0:T(8,128)(2,1)S(1)} %get-tuple-element.67, bf16[1,256,2048]{2,1,0:T(8,128)(2,1)} %collective-permute-done), kind=kLoop, calls=%fused_computation.31 | loop fusion | flops 17301504 | bytes 23068672 | tf_op jit(solution)/shard_map/concatenate | solution.py:116
  300.3 10.0 %fusion.117 = (bf16[2816,1024]{1,0:T(8,128)(2,1)}, bf16[2816,1024]{1,0:T(8,128)(2,1)}) fusion(bf16[2816,2048]{1,0:T(8,128)(2,1)} %bitcast.139), kind=kLoop, calls=%fused_computation.134 | loop fusion | bytes 23068672 | tf_op jit(solution)/shard_map/slice | solution.py:130
  310.4 8.4 %copy.40 = bf16[2816,1024]{0,1:T(8,128)(2,1)} copy(bf16[2816,1024]{1,0:T(8,128)(2,1)} %get-tuple-element.65) | data formatting | bytes 11534336
  318.7 8.4 %copy.39 = bf16[2816,1024]{0,1:T(8,128)(2,1)} copy(bf16[2816,1024]{1,0:T(8,128)(2,1)} %get-tuple-element.66) | data formatting | bytes 11534336
  327.2 63.7 %while.11 = (s32[]{:T(128)}, bf16[4,256,4,64]{1,3,2,0:T(8,128)(2,1)S(1)}, bf16[4,2816,4,64]{1,3,2,0:T(8,128)(2,1)}, pred[11,256]{1,0:T(8,128)(4,1)}, bf16[4,256,...) while((s32[]{:T(128)}, ...), condition=%wide.wide.region_8.9_spmd, body=%wide.wide.region_5.8_spmd.sunk | while | flops 755501824 | bytes 26358620 | solution.py:58
  327.2 9.3 %fusion.134 = (f32[4,256]{1,0:T(4,128)S(1)}, f32[4,256,2816]{2,1,0:T(8,128)}) fusion(pred[2816]{0:T(1024)(128)(4,1)S(1)} %get-tuple-element.174, bf16[4,2816,4,64]{1,3,2,0:T(8,128)(2,1)} %get-tuple-element.173, s32[]{:T(128)S(6)} %copy.71, bf16[4,256,4,64]{1,3,2,0:T(8,128)(2,1)} %get-tuple-element.172), kind=kOutput, calls=%fused_computation.133.clone.clone.1 | convolution fusion | flops 380635904 | bytes 13115136 | tf_op jit(solution)/shard_map/while/body/eval_jaxpr/sub | solution.py:52
  336.5 6.6 %fusion.135 = bf16[4,256,4,64]{1,3,2,0:T(8,128)(2,1)S(1)} fusion(bf16[4,256,4,64]{1,3,2,0:T(8,128)(2,1)S(1)} %get-tuple-element.161, s32[]{:T(128)S(6)} %copy.71, f32[4,256,2816]{2,1,0:T(8,128)} %get-tuple-element.150, f32[4,256]{1,0:T(4,128)S(1)} %get-tuple-element.151, bf16[4,2816,4,64]{1,3,2,0:T(8,128)(2,1)} %get-tuple-element.170), kind=kOutput, calls=%fused_computation.21.clone.clone.1 | convolution fusion | flops 374865920 | bytes 13243392 | tf_op jit(solution)/shard_map/while/body/eval_jaxpr/hqk,khd->qhd/dot_general | solution.py:54
  343.1 9.3 %fusion.134 = (f32[4,256]{1,0:T(4,128)S(1)}, f32[4,256,2816]{2,1,0:T(8,128)}) fusion(pred[2816]{0:T(1024)(128)(4,1)S(1)} %get-tuple-element.174, bf16[4,2816,4,64]{1,3,2,0:T(8,128)(2,1)} %get-tuple-element.173, s32[]{:T(128)S(6)} %copy.71, bf16[4,256,4,64]{1,3,2,0:T(8,128)(2,1)} %get-tuple-element.172), kind=kOutput, calls=%fused_computation.133.clone.clone.1 | convolution fusion | flops 380635904 | bytes 13115136 | tf_op jit(solution)/shard_map/while/body/eval_jaxpr/sub | solution.py:52
  352.4 6.6 %fusion.135 = bf16[4,256,4,64]{1,3,2,0:T(8,128)(2,1)S(1)} fusion(bf16[4,256,4,64]{1,3,2,0:T(8,128)(2,1)S(1)} %get-tuple-element.161, s32[]{:T(128)S(6)} %copy.71, f32[4,256,2816]{2,1,0:T(8,128)} %get-tuple-element.150, f32[4,256]{1,0:T(4,128)S(1)} %get-tuple-element.151, bf16[4,2816,4,64]{1,3,2,0:T(8,128)(2,1)} %get-tuple-element.170), kind=kOutput, calls=%fused_computation.21.clone.clone.1 | convolution fusion | flops 374865920 | bytes 13243392 | tf_op jit(solution)/shard_map/while/body/eval_jaxpr/hqk,khd->qhd/dot_general | solution.py:54
  359.1 9.3 %fusion.134 = (f32[4,256]{1,0:T(4,128)S(1)}, f32[4,256,2816]{2,1,0:T(8,128)}) fusion(pred[2816]{0:T(1024)(128)(4,1)S(1)} %get-tuple-element.174, bf16[4,2816,4,64]{1,3,2,0:T(8,128)(2,1)} %get-tuple-element.173, s32[]{:T(128)S(6)} %copy.71, bf16[4,256,4,64]{1,3,2,0:T(8,128)(2,1)} %get-tuple-element.172), kind=kOutput, calls=%fused_computation.133.clone.clone.1 | convolution fusion | flops 380635904 | bytes 13115136 | tf_op jit(solution)/shard_map/while/body/eval_jaxpr/sub | solution.py:52
  368.3 6.6 %fusion.135 = bf16[4,256,4,64]{1,3,2,0:T(8,128)(2,1)S(1)} fusion(bf16[4,256,4,64]{1,3,2,0:T(8,128)(2,1)S(1)} %get-tuple-element.161, s32[]{:T(128)S(6)} %copy.71, f32[4,256,2816]{2,1,0:T(8,128)} %get-tuple-element.150, f32[4,256]{1,0:T(4,128)S(1)} %get-tuple-element.151, bf16[4,2816,4,64]{1,3,2,0:T(8,128)(2,1)} %get-tuple-element.170), kind=kOutput, calls=%fused_computation.21.clone.clone.1 | convolution fusion | flops 374865920 | bytes 13243392 | tf_op jit(solution)/shard_map/while/body/eval_jaxpr/hqk,khd->qhd/dot_general | solution.py:54
  375.0 9.3 %fusion.134 = (f32[4,256]{1,0:T(4,128)S(1)}, f32[4,256,2816]{2,1,0:T(8,128)}) fusion(pred[2816]{0:T(1024)(128)(4,1)S(1)} %get-tuple-element.174, bf16[4,2816,4,64]{1,3,2,0:T(8,128)(2,1)} %get-tuple-element.173, s32[]{:T(128)S(6)} %copy.71, bf16[4,256,4,64]{1,3,2,0:T(8,128)(2,1)} %get-tuple-element.172), kind=kOutput, calls=%fused_computation.133.clone.clone.1 | convolution fusion | flops 380635904 | bytes 13115136 | tf_op jit(solution)/shard_map/while/body/eval_jaxpr/sub | solution.py:52
  384.2 6.6 %fusion.135 = bf16[4,256,4,64]{1,3,2,0:T(8,128)(2,1)S(1)} fusion(bf16[4,256,4,64]{1,3,2,0:T(8,128)(2,1)S(1)} %get-tuple-element.161, s32[]{:T(128)S(6)} %copy.71, f32[4,256,2816]{2,1,0:T(8,128)} %get-tuple-element.150, f32[4,256]{1,0:T(4,128)S(1)} %get-tuple-element.151, bf16[4,2816,4,64]{1,3,2,0:T(8,128)(2,1)} %get-tuple-element.170), kind=kOutput, calls=%fused_computation.21.clone.clone.1 | convolution fusion | flops 374865920 | bytes 13243392 | tf_op jit(solution)/shard_map/while/body/eval_jaxpr/hqk,khd->qhd/dot_general | solution.py:54
  390.9 1.7 fusion.62
  (26 shorter events, 0.2 us)
Async XLA Ops:
  6.5 384.4 %copy-start = (bf16[1024,1024]{1,0:T(8,128)(2,1)S(1)}, bf16[1024,1024]{1,0:T(8,128)(2,1)}, u32[]{:S(2)}) copy-start(bf16[1024,1024]{1,0:T(8,128)(2,1)} %param.9) | copy-start | bytes 6291460
  6.5 10.6 %copy-start.6 = (s32[8,32,8]{1,2,0:T(8,128)S(1)}, s32[8,32,8]{1,2,0:T(8,128)}, u32[]{:S(2)}) copy-start(s32[8,32,8]{1,2,0:T(8,128)} %param.10) | copy-start | bytes 24580
  6.5 12.1 %copy-start.5 = (s32[8,8192]{1,0:T(8,128)S(1)}, s32[8,8192]{1,0:T(8,128)}, u32[]{:S(2)}) copy-start(s32[8,8192]{1,0:T(8,128)} %param.11) | copy-start | bytes 786436
  6.5 63.9 %all-gather.3.cloned.1.call-start = ((), (), s32[]{:S(2)}) async-start(), calls=%async_computation | async-start | bytes 9437184 | tf_op jit(solution)/shard_map/all_gather | solution.py:110
  11.4 1.2 copy-start.2
  13.8 277.0 %collective-permute-start.1 = (bf16[1,256,2048]{2,1,0:T(8,128)(2,1)S(1)}, bf16[1,256,2048]{2,1,0:T(8,128)(2,1)}, u32[]{:S(2)}, u32[]{:S(2)}) collective-permute-start(bf16[1,256,2048]{2,1,0:T(8,128)(2,1)S(1)} %get-tuple-element.67), channel_id=1, source_target_pairs={{1,0},{2,1},{3,2},{4,3},{5,4},{6,5},{7,6},{8,7},{9,8},{10,9},{11,1... | collective-permute-start | bytes 3145736 | tf_op jit(solution)/shard_map/ppermute | solution.py:22
  20.5 73.9 %copy-start.7 = (pred[11,256]{1,0:T(8,128)(4,1)}, pred[11,256]{1,0:T(8,128)(4,1)S(1)}, u32[]{:S(2)}) copy-start(pred[11,256]{1,0:T(8,128)(4,1)S(1)} %pad_add_fusion) | copy-start | bytes 8452
  70.5 16.9 %copy-start.1 = (bf16[2048,2048]{1,0:T(8,128)(2,1)S(1)}, bf16[2048,2048]{1,0:T(8,128)(2,1)}, u32[]{:S(2)}) copy-start(bf16[2048,2048]{1,0:T(8,128)(2,1)} %all-gather.3.cloned.1.call-done) | copy-start | bytes 25165828
  81.4 49.8 %collective-permute-start.2 = (bf16[2,256,2048]{2,0,1:T(2,128)(2,1)}, bf16[2,256,2048]{2,0,1:T(2,128)(2,1)}, u32[]{:S(2)}, u32[]{:S(2)}) collective-permute-start(bf16[2,256,2048]{2,0,1:T(2,128)(2,1)} %fusion.50), channel_id=1, source_target_pairs={{0,2},{1,3},{2,4},{3,5},{4,6},{5,7},{6,8},{7,9},{8,10},{9,11},{10,... | collective-permute-start | bytes 6291464 | tf_op jit(solution)/shard_map/ppermute | solution.py:32
  94.4 133.6 %collective-permute-start.3 = (bf16[2,256,2048]{2,0,1:T(2,128)(2,1)}, bf16[2,256,2048]{2,0,1:T(2,128)(2,1)}, u32[]{:S(2)}, u32[]{:S(2)}) collective-permute-start(bf16[2,256,2048]{2,0,1:T(2,128)(2,1)} %fusion.53), channel_id=1, source_target_pairs={{0,1},{1,2},{2,3},{3,4},{4,5},{5,6},{6,7},{7,8},{8,9},{9,10},{10,1... | collective-permute-start | bytes 6291464 | tf_op jit(solution)/shard_map/ppermute | solution.py:32
  104.9 162.0 %collective-permute-start.4 = (bf16[2,256,2048]{2,0,1:T(2,128)(2,1)}, bf16[2,256,2048]{2,0,1:T(2,128)(2,1)}, u32[]{:S(2)}, u32[]{:S(2)}) collective-permute-start(bf16[2,256,2048]{2,0,1:T(2,128)(2,1)} %fusion.56), channel_id=1, source_target_pairs={{1,0},{2,1},{3,2},{4,3},{5,4},{6,5},{7,6},{8,7},{9,8},{10,9},{11,1... | collective-permute-start | bytes 6291464 | tf_op jit(solution)/shard_map/ppermute | solution.py:32
  113.2 157.5 %collective-permute-start.5 = (bf16[2,256,2048]{2,0,1:T(2,128)(2,1)}, bf16[2,256,2048]{2,0,1:T(2,128)(2,1)S(1)}, u32[]{:S(2)}, u32[]{:S(2)}) collective-permute-start(bf16[2,256,2048]{2,0,1:T(2,128)(2,1)} %fusion.59), channel_id=1, source_target_pairs={{2,0},{3,1},{4,2},{5,3},{6,4},{7,5},{8,6},{9,7},{10,8},{11,9},{12,... | collective-permute-start | bytes 6291464 | tf_op jit(solution)/shard_map/ppermute | solution.py:32
  131.2 159.7 %collective-permute-start = (bf16[1,256,2048]{2,1,0:T(8,128)(2,1)S(1)}, bf16[1,256,2048]{2,1,0:T(8,128)(2,1)}, u32[]{:S(2)}, u32[]{:S(2)}) collective-permute-start(bf16[1,256,2048]{2,1,0:T(8,128)(2,1)S(1)} %get-tuple-element.67), channel_id=1, source_target_pairs={{0,1},{1,2},{2,3},{3,4},{4,5},{5,6},{6,7},{7,8},{8,9},{9,10},{10,1... | collective-permute-start | bytes 3145736 | tf_op jit(solution)/shard_map/ppermute | solution.py:20
  318.7 8.4 %copy-start.4 = (bf16[4,256,4,64]{1,3,2,0:T(8,128)(2,1)S(1)}, bf16[4,256,4,64]{1,3,2,0:T(8,128)(2,1)}, u32[]{:S(2)}) copy-start(bf16[4,256,4,64]{1,3,2,0:T(8,128)(2,1)} %custom-call.7) | copy-start | bytes 1572868
  327.2 63.7 %copy-start.3 = (bf16[1,256,1024]{2,1,0:T(8,128)(2,1)S(1)}, bf16[1,256,1024]{2,1,0:T(8,128)(2,1)}, u32[]{:S(2)}) copy-start(bf16[1,256,1024]{2,1,0:T(8,128)(2,1)} %param.7) | copy-start | bytes 1572868
Sparse Core Ops, SparseCore 0:
  14.0 56.4 all-gather.2
where the time goes:
time: 401 us; the launch traced here: 399 us
  starting transfers between devices  106 us (26%)
  matrix products  102 us (25%)
  waiting for transfers between devices  91.4 us (23%)
  local copies, waits for them, and re-layouts  66.8 us (17%)
  other arithmetic  19.1 us (5%)
  between operations  13.6 us (3%)
    ppermute x1, starting transfers between devices, with_halo(): lax.ppermute(tail, axis, [(i, (i + 1) % count) for i in range(ends)])  93 us
    all_gather x1, waiting for transfers between devices, body(): gathered = lax.all_gather(key_value[None], 'view', axis=0, tiled=True)  47.9 us
    ppermute x4, waiting for transfers between devices, from_behind(): return lax.ppermute(block, axis, route)  43.5 us
    unnamed x23, local copies, waits for them, and re-layouts  37.8 us
    sub x4, matrix products, per_group(): raised = jnp.exp(scores - row_top)  37 us
    dot_general x4, matrix products, offset_payload(): jnp.einsum('rw,wtc->rtc', picker, pick_from, preferred_element_type=jnp.f...  31.9 us
    dot_general x4, matrix products, per_group(): jnp.einsum('hqk,khd->qhd', attention, value_block, preferred_element_type...  26.6 us
    ppermute x4, starting transfers between devices, from_behind(): return lax.ppermute(block, axis, route)  12.1 us
  transfers between devices with their start and end apart: 7, of which 3 were waited for; matrix products, arithmetic and copies ran while one was open for 20% of the time, Pallas kernels for 0%

commit v1 on v0

--- a/solution.py
+++ b/solution.py
@@ -107,7 +107,23 @@
     view_numbers = jnp.arange(view_list, dtype=jnp.int32)
     nonzero = [distance_step for distance_step in range(-REACH, REACH + 1) if distance_step != 0]
     nearby = with_halo(key_value[None], (("band", 0),), 1)
-    gathered = lax.all_gather(key_value[None], "view", axis=0, tiled=True)
+    ways, here, step = (lax.axis_size("view"), lax.axis_index("view"), key_value[None].shape[0])
+    shape = [n * ways if d == 0 else n for d, n in enumerate(key_value[None].shape)]
+    full = lax.dynamic_update_slice_in_dim(
+        jnp.zeros(shape, key_value[None].dtype), key_value[None], here * step, axis=0
+    )
+    going_up = going_down = key_value[None]
+    for far in range(1, ways // 2 + 1):
+        going_up = lax.ppermute(going_up, "view", [(d, (d + 1) % ways) for d in range(ways)])
+        full = lax.dynamic_update_slice_in_dim(full, going_up, (here - far) % ways * step, axis=0)
+        if 2 * far < ways:
+            going_down = lax.ppermute(
+                going_down, "view", [(d, (d - 1) % ways) for d in range(ways)]
+            )
+            full = lax.dynamic_update_slice_in_dim(
+                full, going_down, (here + far) % ways * step, axis=0
+            )
+    gathered = full
     sources = [gathered]
     for offset in nonzero:
         payload = offset_payload(offset, gathered, epipolar_bands, local_view, my_band, band_list)

time: 401 us -> 386 us (0.963)
  the two profiles are of different devices: /device:TPU:1 before, /device:TPU:7 now
where the time goes in v1:
time: 386 us; the launch traced here: 384 us
  starting transfers between devices  121 us (31%)
  matrix products  98.2 us (25%)
  waiting for transfers between devices  74.4 us (19%)
  local copies, waits for them, and re-layouts  71.4 us (18%)
  other arithmetic  19.1 us (5%)
    ppermute x1, starting transfers between devices, with_halo(): lax.ppermute(tail, axis, [(i, (i + 1) % count) for i in range(ends)])  93 us
    ppermute x4, waiting for transfers between devices, from_behind(): return lax.ppermute(block, axis, route)  41.1 us
    sub x4, matrix products, per_group(): raised = jnp.exp(scores - row_top)  37.1 us
    dot_general x4, matrix products, offset_payload(): jnp.einsum('rw,wtc->rtc', picker, pick_from, preferred_element_type=jnp.f...  28 us
    ppermute x4, waiting for transfers between devices, body(): lax.ppermute(going_up, 'view', [(d, (d + 1) % ways) for d in range(ways)])  27.3 us
    dot_general x4, matrix products, per_group(): jnp.einsum('hqk,khd->qhd', attention, value_block, preferred_element_type...  26.6 us
    unnamed x23, local copies, waits for them, and re-layouts  21 us
    slice x2, local copies, waits for them, and re-layouts, body(): flattened[:, :width]  18.4 us
  transfers between devices with their start and end apart: 13, of which 8 were waited for; matrix products, arithmetic and copies ran while one was open for 21% of the time, Pallas kernels for 0%

profile of v1, /device:TPU:7, one launch (start us, length us, event | category | flops | bytes accessed | tf_op | source)
XLA Modules:
  0.0 384.4 jit_solution(6687721553344825550)
XLA Ops:
  0.0 4.9 %convolution_convert_fusion = bf16[256,3072]{1,0:T(8,128)(2,1)S(1)} fusion(bf16[1024,3072]{1,0:T(8,128)(2,1)} %param.8, bf16[1,256,1024]{2,1,0:T(8,128)(2,1)} %param.7), kind=kOutput, calls=%fused_computation.41 | convolution fusion | flops 1611399168 | bytes 8388608 | tf_op jit(solution)/shard_map/dot_general | solution.py:102
  4.9 1.1 copy-done.2
  6.1 0.7 collective-permute-start.3
  6.8 2.3 collective-permute-start.2
  9.1 1.3 collective-permute-start.1
  10.6 0.2 compare_reduce_fusion
  10.8 0.3 clamp_reduce_fusion
  11.1 0.2 convert_reduce_fusion.4
  11.3 0.6 gather_fusion.2
  12.0 0.6 gather_fusion.1
  12.6 8.3 %collective-permute-done.2 = bf16[1,256,2048]{2,1,0:T(8,128)(2,1)} collective-permute-done((bf16[1,256,2048]{2,1,0:T(8,128)(2,1)S(1)}, bf16[1,256,2048]{2,1,0:T(8,128)(2,1)}, u32[]{:S(2)}, u32[]{:S(2)}) %collective-permute-start.2) | collective-permute-done | bytes 1048608 | tf_op jit(solution)/shard_map/ppermute | solution.py:117
  20.9 3.8 collective-permute-start.4
  24.7 1.9 slice.24
  26.6 0.1 reduce.4
  26.7 0.1 reduce.2
  26.9 0.1 reduce.8
  27.1 0.2 reduce-window.33
  27.3 0.2 reduce-window.32
  27.5 0.2 reduce-window.35
  27.6 0.2 reduce-window.34
  27.9 2.0 copy.49
  30.0 6.7 %collective-permute-done.4 = bf16[1,256,2048]{2,1,0:T(8,128)(2,1)} collective-permute-done((bf16[1,256,2048]{2,1,0:T(8,128)(2,1)}, bf16[1,256,2048]{2,1,0:T(8,128)(2,1)}, u32[]{:S(2)}, u32[]{:S(2)}) %collective-permute-start.4) | collective-permute-done | bytes 1048608 | tf_op jit(solution)/shard_map/ppermute | solution.py:117
  36.7 3.7 collective-permute-start.6
  40.4 1.1 broadcast_in_dim.36
  41.6 4.0 %collective-permute-done.5 = bf16[1,256,2048]{2,1,0:T(8,128)(2,1)S(1)} collective-permute-done((bf16[1,256,2048]{2,1,0:T(8,128)(2,1)}, bf16[1,256,2048]{2,1,0:T(8,128)(2,1)S(1)}, u32[]{:S(2)}, u32[]{:S(2)}) %collective-permute-start.5) | collective-permute-done | bytes 1048608 | tf_op jit(solution)/shard_map/ppermute | solution.py:120
  45.6 1.3 constant_dynamic-update-slice_fusion.7
  46.9 5.5 %collective-permute-done.6 = bf16[1,256,2048]{2,1,0:T(8,128)(2,1)S(1)} collective-permute-done((bf16[1,256,2048]{2,1,0:T(8,128)(2,1)}, bf16[1,256,2048]{2,1,0:T(8,128)(2,1)S(1)}, u32[]{:S(2)}, u32[]{:S(2)}) %collective-permute-start.6) | collective-permute-done | bytes 1048608 | tf_op jit(solution)/shard_map/ppermute | solution.py:117
  52.5 3.6 collective-permute-start.8
  56.1 1.3 constant_dynamic-update-slice_fusion.6
  57.4 1.3 constant_dynamic-update-slice_fusion.5
  59.0 2.0 collective-permute-done.7
  61.1 6.7 %collective-permute-done.8 = bf16[1,256,2048]{2,1,0:T(8,128)(2,1)S(1)} collective-permute-done((bf16[1,256,2048]{2,1,0:T(8,128)(2,1)S(1)}, bf16[1,256,2048]{2,1,0:T(8,128)(2,1)S(1)}, u32[]{:S(2)}, u32[]{:S(2)}) %collective-permute-start.8) | collective-permute-done | bytes 1048608 | tf_op jit(solution)/shard_map/ppermute | solution.py:117
  67.9 7.0 %fusion.50 = bf16[2,256,2048]{2,0,1:T(2,128)(2,1)} fusion(bf16[8,256,2048]{2,1,0:T(8,128)(2,1)S(1)} %constant_dynamic-update-slice_fusion.1, pred[8]{0:T(512)(128)(4,1)S(1)} %reduce.2, s32[8]{0:T(128)S(1)} %bitcast_subtract_fusion.3), kind=kOutput, calls=%fused_computation.42 | convolution fusion | flops 17825824 | bytes 10485800 | tf_op jit(solution)/shard_map/rw,wtc->rtc/dot_general | solution.py:73
  74.9 6.2 %collective-permute-start.9 = (bf16[2,256,2048]{2,0,1:T(2,128)(2,1)}, bf16[2,256,2048]{2,0,1:T(2,128)(2,1)}, u32[]{:S(2)}, u32[]{:S(2)}) collective-permute-start(bf16[2,256,2048]{2,0,1:T(2,128)(2,1)} %fusion.50), channel_id=1, source_target_pairs={{0,2},{1,3},{2,4},{3,5},{4,6},{5,7},{6,8},{7,9},{8,10},{9,11},{10,... | collective-permute-start | bytes 6291464 | tf_op jit(solution)/shard_map/ppermute | solution.py:32
  81.1 7.0 %fusion.53 = bf16[2,256,2048]{2,0,1:T(2,128)(2,1)} fusion(bf16[8,256,2048]{2,1,0:T(8,128)(2,1)S(1)} %constant_dynamic-update-slice_fusion.1, pred[8]{0:T(512)(128)(4,1)S(1)} %reduce.4, s32[8]{0:T(128)S(1)} %bitcast_subtract_fusion.2), kind=kOutput, calls=%fused_computation.43 | convolution fusion | flops 17825824 | bytes 10485800 | tf_op jit(solution)/shard_map/rw,wtc->rtc/dot_general | solution.py:73
  88.1 3.6 collective-permute-start.10
  91.7 7.0 %fusion.56 = bf16[2,256,2048]{2,0,1:T(2,128)(2,1)} fusion(bf16[8,256,2048]{2,1,0:T(8,128)(2,1)S(1)} %constant_dynamic-update-slice_fusion.1, pred[8]{0:T(512)(128)(4,1)S(1)} %reduce.6, s32[8]{0:T(128)S(1)} %bitcast_subtract_fusion.1), kind=kOutput, calls=%fused_computation.44 | convolution fusion | flops 17825824 | bytes 10485800 | tf_op jit(solution)/shard_map/rw,wtc->rtc/dot_general | solution.py:73
  98.7 1.3 collective-permute-start.11
  100.0 7.0 %fusion.59 = bf16[2,256,2048]{2,0,1:T(2,128)(2,1)} fusion(bf16[8,256,2048]{2,1,0:T(8,128)(2,1)S(1)} %constant_dynamic-update-slice_fusion.1, pred[8]{0:T(512)(128)(4,1)S(1)} %reduce.8, s32[8]{0:T(128)S(1)} %bitcast_subtract_fusion), kind=kOutput, calls=%fused_computation.45 | convolution fusion | flops 17825824 | bytes 10485800 | tf_op jit(solution)/shard_map/rw,wtc->rtc/dot_general | solution.py:73
  107.0 1.3 collective-permute-start.12
  108.3 8.3 %constant_dynamic-update-slice_fusion = bf16[16,256,2048]{2,1,0:T(8,128)(2,1)} fusion(bf16[8,256,2048]{2,1,0:T(8,128)(2,1)} %copy-done.1), kind=kLoop, calls=%fused_computation.57 | loop fusion | bytes 16777216
  116.6 9.0 %collective-permute-done.9 = bf16[2,256,2048]{2,0,1:T(2,128)(2,1)} collective-permute-done((bf16[2,256,2048]{2,0,1:T(2,128)(2,1)}, bf16[2,256,2048]{2,0,1:T(2,128)(2,1)}, u32[]{:S(2)}, u32[]{:S(2)}) %collective-permute-start.9) | collective-permute-done | bytes 2097184 | tf_op jit(solution)/shard_map/ppermute | solution.py:32
  125.6 93.0 %collective-permute-start = (bf16[1,256,2048]{2,1,0:T(8,128)(2,1)S(1)}, bf16[1,256,2048]{2,1,0:T(8,128)(2,1)}, u32[]{:S(2)}, u32[]{:S(2)}) collective-permute-start(bf16[1,256,2048]{2,1,0:T(8,128)(2,1)S(1)} %slice_bitcast_fusion), channel_id=1, source_target_pairs={{0,1},{1,2},{2,3},{3,4},{4,5},{5,6},{6,7},{7,8},{8,9},{9,10},{10,1... | collective-permute-start | bytes 3145736 | tf_op jit(solution)/shard_map/ppermute | solution.py:20
  218.6 3.9 %copy_dynamic-update-slice_fusion.3 = bf16[16,256,2048]{2,1,0:T(8,128)(2,1)} fusion(bf16[16,256,2048]{2,1,0:T(8,128)(2,1)} %constant_dynamic-update-slice_fusion, bf16[2,256,2048]{2,0,1:T(2,128)(2,1)} %collective-permute-done.9), kind=kLoop, calls=%fused_computation.49 | loop fusion | bytes 4194304
  222.5 3.8 copy_dynamic-update-slice_fusion.2
  226.3 32.1 %collective-permute-done.11 = bf16[2,256,2048]{2,0,1:T(2,128)(2,1)} collective-permute-done((bf16[2,256,2048]{2,0,1:T(2,128)(2,1)}, bf16[2,256,2048]{2,0,1:T(2,128)(2,1)}, u32[]{:S(2)}, u32[]{:S(2)}) %collective-permute-start.11) | collective-permute-done | bytes 2097184 | tf_op jit(solution)/shard_map/ppermute | solution.py:32
  258.4 3.8 copy_dynamic-update-slice_fusion.1
  262.2 2.2 copy_dynamic-update-slice_fusion
  264.4 10.7 %gather_fusion = bf16[8,256,2048]{2,1,0:T(8,128)(2,1)} fusion(bf16[16,256,2048]{2,1,0:T(8,128)(2,1)} %copy_dynamic-update-slice_fusion, s32[1024]{0:T(1024)S(1)} %pad_clamp_fusion), kind=kCustom, calls=%fused_computation | custom fusion | bytes 16777248 | tf_op jit(solution)/shard_map/jit(_take)/gather | solution.py:91
  275.1 7.5 %broadcast_select_fusion = bf16[8,256,2048]{2,1,0:T(8,128)(2,1)} fusion(bf16[8,256,2048]{2,1,0:T(8,128)(2,1)} %gather_fusion, pred[8]{0:T(512)(128)(4,1)S(1)} %compare_and_fusion.1), kind=kLoop, calls=%fused_computation.32 | loop fusion | flops 4194304 | bytes 16777224 | tf_op jit(solution)/shard_map/jit(_take)/select_n | solution.py:91
  282.6 9.5 %pad_maximum_fusion = bf16[11,256,2048]{2,1,0:T(8,128)(2,1)} fusion(bf16[8,256,2048]{2,1,0:T(8,128)(2,1)} %broadcast_select_fusion, bf16[1,256,2048]{2,1,0:T(8,128)(2,1)} %collective-permute-done.1, bf16[1,256,2048]{2,1,0:T(8,128)(2,1)S(1)} %slice_bitcast_fusion, bf16[1,256,2048]{2,1,0:T(8,128)(2,1)} %collective-permute-done), kind=kLoop, calls=%fused_computation.31 | loop fusion | flops 17301504 | bytes 23068672 | tf_op jit(solution)/shard_map/concatenate | solution.py:132
  292.1 10.0 %fusion.117 = (bf16[2816,1024]{1,0:T(8,128)(2,1)}, bf16[2816,1024]{1,0:T(8,128)(2,1)}) fusion(bf16[2816,2048]{1,0:T(8,128)(2,1)} %bitcast.135), kind=kLoop, calls=%fused_computation.142 | loop fusion | bytes 23068672 | tf_op jit(solution)/shard_map/slice | solution.py:146
  302.1 8.4 %copy.50 = bf16[2816,1024]{0,1:T(8,128)(2,1)} copy(bf16[2816,1024]{1,0:T(8,128)(2,1)} %get-tuple-element.65) | data formatting | bytes 11534336 | tf_op jit(solution)/shard_map/slice | solution.py:146
  310.5 8.4 %copy.48 = bf16[2816,1024]{0,1:T(8,128)(2,1)} copy(bf16[2816,1024]{1,0:T(8,128)(2,1)} %get-tuple-element.66) | data formatting | bytes 11534336 | tf_op jit(solution)/shard_map/slice | solution.py:146
  318.9 63.7 %while.11 = (s32[]{:T(128)}, bf16[4,256,4,64]{1,3,2,0:T(8,128)(2,1)S(1)}, bf16[4,2816,4,64]{1,3,2,0:T(8,128)(2,1)}, pred[11,256]{1,0:T(8,128)(4,1)}, bf16[4,256,...) while((s32[]{:T(128)}, ...), condition=%wide.wide.region_8.9_spmd, body=%wide.wide.region_5.8_spmd.sunk | while | flops 755501824 | bytes 26358620 | solution.py:58
  318.9 9.3 %fusion.134 = (f32[4,256]{1,0:T(4,128)S(1)}, f32[4,256,2816]{2,1,0:T(8,128)}) fusion(pred[2816]{0:T(1024)(128)(4,1)S(1)} %get-tuple-element.172, bf16[4,2816,4,64]{1,3,2,0:T(8,128)(2,1)} %get-tuple-element.171, s32[]{:T(128)S(6)} %copy.89, bf16[4,256,4,64]{1,3,2,0:T(8,128)(2,1)} %get-tuple-element.170), kind=kOutput, calls=%fused_computation.141.clone.clone.1 | convolution fusion | flops 380635904 | bytes 13115136 | tf_op jit(solution)/shard_map/while/body/eval_jaxpr/sub | solution.py:52
  328.2 6.6 %fusion.135 = bf16[4,256,4,64]{1,3,2,0:T(8,128)(2,1)S(1)} fusion(bf16[4,256,4,64]{1,3,2,0:T(8,128)(2,1)S(1)} %get-tuple-element.159, s32[]{:T(128)S(6)} %copy.89, f32[4,256,2816]{2,1,0:T(8,128)} %get-tuple-element.148, f32[4,256]{1,0:T(4,128)S(1)} %get-tuple-element.149, bf16[4,2816,4,64]{1,3,2,0:T(8,128)(2,1)} %get-tuple-element.168), kind=kOutput, calls=%fused_computation.21.clone.clone.1 | convolution fusion | flops 374865920 | bytes 13243392 | tf_op jit(solution)/shard_map/while/body/eval_jaxpr/hqk,khd->qhd/dot_general | solution.py:54
  334.9 9.3 %fusion.134 = (f32[4,256]{1,0:T(4,128)S(1)}, f32[4,256,2816]{2,1,0:T(8,128)}) fusion(pred[2816]{0:T(1024)(128)(4,1)S(1)} %get-tuple-element.172, bf16[4,2816,4,64]{1,3,2,0:T(8,128)(2,1)} %get-tuple-element.171, s32[]{:T(128)S(6)} %copy.89, bf16[4,256,4,64]{1,3,2,0:T(8,128)(2,1)} %get-tuple-element.170), kind=kOutput, calls=%fused_computation.141.clone.clone.1 | convolution fusion | flops 380635904 | bytes 13115136 | tf_op jit(solution)/shard_map/while/body/eval_jaxpr/sub | solution.py:52
  344.1 6.6 %fusion.135 = bf16[4,256,4,64]{1,3,2,0:T(8,128)(2,1)S(1)} fusion(bf16[4,256,4,64]{1,3,2,0:T(8,128)(2,1)S(1)} %get-tuple-element.159, s32[]{:T(128)S(6)} %copy.89, f32[4,256,2816]{2,1,0:T(8,128)} %get-tuple-element.148, f32[4,256]{1,0:T(4,128)S(1)} %get-tuple-element.149, bf16[4,2816,4,64]{1,3,2,0:T(8,128)(2,1)} %get-tuple-element.168), kind=kOutput, calls=%fused_computation.21.clone.clone.1 | convolution fusion | flops 374865920 | bytes 13243392 | tf_op jit(solution)/shard_map/while/body/eval_jaxpr/hqk,khd->qhd/dot_general | solution.py:54
  350.8 9.3 %fusion.134 = (f32[4,256]{1,0:T(4,128)S(1)}, f32[4,256,2816]{2,1,0:T(8,128)}) fusion(pred[2816]{0:T(1024)(128)(4,1)S(1)} %get-tuple-element.172, bf16[4,2816,4,64]{1,3,2,0:T(8,128)(2,1)} %get-tuple-element.171, s32[]{:T(128)S(6)} %copy.89, bf16[4,256,4,64]{1,3,2,0:T(8,128)(2,1)} %get-tuple-element.170), kind=kOutput, calls=%fused_computation.141.clone.clone.1 | convolution fusion | flops 380635904 | bytes 13115136 | tf_op jit(solution)/shard_map/while/body/eval_jaxpr/sub | solution.py:52
  360.1 6.6 %fusion.135 = bf16[4,256,4,64]{1,3,2,0:T(8,128)(2,1)S(1)} fusion(bf16[4,256,4,64]{1,3,2,0:T(8,128)(2,1)S(1)} %get-tuple-element.159, s32[]{:T(128)S(6)} %copy.89, f32[4,256,2816]{2,1,0:T(8,128)} %get-tuple-element.148, f32[4,256]{1,0:T(4,128)S(1)} %get-tuple-element.149, bf16[4,2816,4,64]{1,3,2,0:T(8,128)(2,1)} %get-tuple-element.168), kind=kOutput, calls=%fused_computation.21.clone.clone.1 | convolution fusion | flops 374865920 | bytes 13243392 | tf_op jit(solution)/shard_map/while/body/eval_jaxpr/hqk,khd->qhd/dot_general | solution.py:54
  366.7 9.3 %fusion.134 = (f32[4,256]{1,0:T(4,128)S(1)}, f32[4,256,2816]{2,1,0:T(8,128)}) fusion(pred[2816]{0:T(1024)(128)(4,1)S(1)} %get-tuple-element.172, bf16[4,2816,4,64]{1,3,2,0:T(8,128)(2,1)} %get-tuple-element.171, s32[]{:T(128)S(6)} %copy.89, bf16[4,256,4,64]{1,3,2,0:T(8,128)(2,1)} %get-tuple-element.170), kind=kOutput, calls=%fused_computation.141.clone.clone.1 | convolution fusion | flops 380635904 | bytes 13115136 | tf_op jit(solution)/shard_map/while/body/eval_jaxpr/sub | solution.py:52
  376.0 6.6 %fusion.135 = bf16[4,256,4,64]{1,3,2,0:T(8,128)(2,1)S(1)} fusion(bf16[4,256,4,64]{1,3,2,0:T(8,128)(2,1)S(1)} %get-tuple-element.159, s32[]{:T(128)S(6)} %copy.89, f32[4,256,2816]{2,1,0:T(8,128)} %get-tuple-element.148, f32[4,256]{1,0:T(4,128)S(1)} %get-tuple-element.149, bf16[4,2816,4,64]{1,3,2,0:T(8,128)(2,1)} %get-tuple-element.168), kind=kOutput, calls=%fused_computation.21.clone.clone.1 | convolution fusion | flops 374865920 | bytes 13243392 | tf_op jit(solution)/shard_map/while/body/eval_jaxpr/hqk,khd->qhd/dot_general | solution.py:54
  382.7 1.7 fusion.62
  (48 shorter events, 1.1 us)
Async XLA Ops:
  0.0 382.7 %copy-start = (bf16[1024,1024]{1,0:T(8,128)(2,1)S(1)}, bf16[1024,1024]{1,0:T(8,128)(2,1)}, u32[]{:S(2)}) copy-start(bf16[1024,1024]{1,0:T(8,128)(2,1)} %param.9) | copy-start | bytes 6291460
  0.0 10.4 %copy-start.6 = (s32[8,8192]{1,0:T(8,128)S(1)}, s32[8,8192]{1,0:T(8,128)}, u32[]{:S(2)}) copy-start(s32[8,8192]{1,0:T(8,128)} %param.11) | copy-start | bytes 786436
  0.0 10.5 %copy-start.7 = (s32[8,32,8]{1,2,0:T(8,128)S(1)}, s32[8,32,8]{1,2,0:T(8,128)}, u32[]{:S(2)}) copy-start(s32[8,32,8]{1,2,0:T(8,128)} %param.10) | copy-start | bytes 24580
  4.9 1.2 copy-start.2
  6.1 23.8 %collective-permute-start.3 = (bf16[1,256,2048]{2,1,0:T(8,128)(2,1)S(1)}, bf16[1,256,2048]{2,1,0:T(8,128)(2,1)}, u32[]{:S(2)}, u32[]{:S(2)}) collective-permute-start(bf16[1,256,2048]{2,1,0:T(8,128)(2,1)S(1)} %slice_bitcast_fusion), channel_id=1, source_target_pairs={{0,224},{32,0},{64,32},{96,64},{128,96},{160,128},{192,160},{224,1... | collective-permute-start | bytes 3145736 | tf_op jit(solution)/shard_map/ppermute | solution.py:120
  6.8 14.0 %collective-permute-start.2 = (bf16[1,256,2048]{2,1,0:T(8,128)(2,1)S(1)}, bf16[1,256,2048]{2,1,0:T(8,128)(2,1)}, u32[]{:S(2)}, u32[]{:S(2)}) collective-permute-start(bf16[1,256,2048]{2,1,0:T(8,128)(2,1)S(1)} %slice_bitcast_fusion), channel_id=1, source_target_pairs={{0,32},{32,64},{64,96},{96,128},{128,160},{160,192},{192,224},{224... | collective-permute-start | bytes 3145736 | tf_op jit(solution)/shard_map/ppermute | solution.py:117
  9.1 273.5 %collective-permute-start.1 = (bf16[1,256,2048]{2,1,0:T(8,128)(2,1)S(1)}, bf16[1,256,2048]{2,1,0:T(8,128)(2,1)}, u32[]{:S(2)}, u32[]{:S(2)}) collective-permute-start(bf16[1,256,2048]{2,1,0:T(8,128)(2,1)S(1)} %slice_bitcast_fusion), channel_id=1, source_target_pairs={{1,0},{2,1},{3,2},{4,3},{5,4},{6,5},{7,6},{8,7},{9,8},{10,9},{11,1... | collective-permute-start | bytes 3145736 | tf_op jit(solution)/shard_map/ppermute | solution.py:22
  20.9 15.9 %collective-permute-start.4 = (bf16[1,256,2048]{2,1,0:T(8,128)(2,1)}, bf16[1,256,2048]{2,1,0:T(8,128)(2,1)}, u32[]{:S(2)}, u32[]{:S(2)}) collective-permute-start(bf16[1,256,2048]{2,1,0:T(8,128)(2,1)} %collective-permute-done.2), channel_id=1, source_target_pairs={{0,32},{32,64},{64,96},{96,128},{128,160},{160,192},{192,224},{224... | collective-permute-start | bytes 3145736 | tf_op jit(solution)/shard_map/ppermute | solution.py:117
  27.8 30.9 %copy-start.8 = (pred[11,256]{1,0:T(8,128)(4,1)}, pred[11,256]{1,0:T(8,128)(4,1)S(1)}, u32[]{:S(2)}) copy-start(pred[11,256]{1,0:T(8,128)(4,1)S(1)} %pad_add_fusion) | copy-start | bytes 8452
  29.9 11.6 %copy-start.3 = (bf16[256,3072]{1,0:T(8,128)(2,1)S(1)}, bf16[256,3072]{1,0:T(8,128)(2,1)}, u32[]{:S(2)}) copy-start(bf16[256,3072]{1,0:T(8,128)(2,1)} %copy-done.2) | copy-start | bytes 4718596
  29.9 15.7 %collective-permute-start.5 = (bf16[1,256,2048]{2,1,0:T(8,128)(2,1)}, bf16[1,256,2048]{2,1,0:T(8,128)(2,1)S(1)}, u32[]{:S(2)}, u32[]{:S(2)}) collective-permute-start(bf16[1,256,2048]{2,1,0:T(8,128)(2,1)} %collective-permute-done.3), channel_id=1, source_target_pairs={{0,224},{32,0},{64,32},{96,64},{128,96},{160,128},{192,160},{224,1... | collective-permute-start | bytes 3145736 | tf_op jit(solution)/shard_map/ppermute | solution.py:120
  36.7 15.8 %collective-permute-start.6 = (bf16[1,256,2048]{2,1,0:T(8,128)(2,1)}, bf16[1,256,2048]{2,1,0:T(8,128)(2,1)S(1)}, u32[]{:S(2)}, u32[]{:S(2)}) collective-permute-start(bf16[1,256,2048]{2,1,0:T(8,128)(2,1)} %collective-permute-done.4), channel_id=1, source_target_pairs={{0,32},{32,64},{64,96},{96,128},{128,160},{160,192},{192,224},{224... | collective-permute-start | bytes 3145736 | tf_op jit(solution)/shard_map/ppermute | solution.py:117
  45.6 15.4 %collective-permute-start.7 = (bf16[1,256,2048]{2,1,0:T(8,128)(2,1)S(1)}, bf16[1,256,2048]{2,1,0:T(8,128)(2,1)S(1)}, u32[]{:S(2)}, u32[]{:S(2)}) collective-permute-start(bf16[1,256,2048]{2,1,0:T(8,128)(2,1)S(1)} %collective-permute-done.5), channel_id=1, source_target_pairs={{0,224},{32,0},{64,32},{96,64},{128,96},{160,128},{192,160},{224,1... | collective-permute-start | bytes 3145736 | tf_op jit(solution)/shard_map/ppermute | solution.py:120
  52.5 15.3 %collective-permute-start.8 = (bf16[1,256,2048]{2,1,0:T(8,128)(2,1)S(1)}, bf16[1,256,2048]{2,1,0:T(8,128)(2,1)S(1)}, u32[]{:S(2)}, u32[]{:S(2)}) collective-permute-start(bf16[1,256,2048]{2,1,0:T(8,128)(2,1)S(1)} %collective-permute-done.6), channel_id=1, source_target_pairs={{0,32},{32,64},{64,96},{96,128},{128,160},{160,192},{192,224},{224... | collective-permute-start | bytes 3145736 | tf_op jit(solution)/shard_map/ppermute | solution.py:117
  67.9 32.1 %copy-start.1 = (bf16[8,256,2048]{2,1,0:T(8,128)(2,1)}, bf16[8,256,2048]{2,1,0:T(8,128)(2,1)S(1)}, u32[]{:S(2)}) copy-start(bf16[8,256,2048]{2,1,0:T(8,128)(2,1)S(1)} %constant_dynamic-update-slice_fusion.1) | copy-start | bytes 25165828
  74.9 50.7 %collective-permute-start.9 = (bf16[2,256,2048]{2,0,1:T(2,128)(2,1)}, bf16[2,256,2048]{2,0,1:T(2,128)(2,1)}, u32[]{:S(2)}, u32[]{:S(2)}) collective-permute-start(bf16[2,256,2048]{2,0,1:T(2,128)(2,1)} %fusion.50), channel_id=1, source_target_pairs={{0,2},{1,3},{2,4},{3,5},{4,6},{5,7},{6,8},{7,9},{8,10},{9,11},{10,... | collective-permute-start | bytes 6291464 | tf_op jit(solution)/shard_map/ppermute | solution.py:32
  88.1 134.4 %collective-permute-start.10 = (bf16[2,256,2048]{2,0,1:T(2,128)(2,1)}, bf16[2,256,2048]{2,0,1:T(2,128)(2,1)}, u32[]{:S(2)}, u32[]{:S(2)}) collective-permute-start(bf16[2,256,2048]{2,0,1:T(2,128)(2,1)} %fusion.53), channel_id=1, source_target_pairs={{0,1},{1,2},{2,3},{3,4},{4,5},{5,6},{6,7},{7,8},{8,9},{9,10},{10,1... | collective-permute-start | bytes 6291464 | tf_op jit(solution)/shard_map/ppermute | solution.py:32
  98.7 159.7 %collective-permute-start.11 = (bf16[2,256,2048]{2,0,1:T(2,128)(2,1)}, bf16[2,256,2048]{2,0,1:T(2,128)(2,1)}, u32[]{:S(2)}, u32[]{:S(2)}) collective-permute-start(bf16[2,256,2048]{2,0,1:T(2,128)(2,1)} %fusion.56), channel_id=1, source_target_pairs={{1,0},{2,1},{3,2},{4,3},{5,4},{6,5},{7,6},{8,7},{9,8},{10,9},{11,1... | collective-permute-start | bytes 6291464 | tf_op jit(solution)/shard_map/ppermute | solution.py:32
  107.0 155.2 %collective-permute-start.12 = (bf16[2,256,2048]{2,0,1:T(2,128)(2,1)}, bf16[2,256,2048]{2,0,1:T(2,128)(2,1)S(1)}, u32[]{:S(2)}, u32[]{:S(2)}) collective-permute-start(bf16[2,256,2048]{2,0,1:T(2,128)(2,1)} %fusion.59), channel_id=1, source_target_pairs={{2,0},{3,1},{4,2},{5,3},{6,4},{7,5},{8,6},{9,7},{10,8},{11,9},{12,... | collective-permute-start | bytes 6291464 | tf_op jit(solution)/shard_map/ppermute | solution.py:32
  125.6 157.0 %collective-permute-start = (bf16[1,256,2048]{2,1,0:T(8,128)(2,1)S(1)}, bf16[1,256,2048]{2,1,0:T(8,128)(2,1)}, u32[]{:S(2)}, u32[]{:S(2)}) collective-permute-start(bf16[1,256,2048]{2,1,0:T(8,128)(2,1)S(1)} %slice_bitcast_fusion), channel_id=1, source_target_pairs={{0,1},{1,2},{2,3},{3,4},{4,5},{5,6},{6,7},{7,8},{8,9},{9,10},{10,1... | collective-permute-start | bytes 3145736 | tf_op jit(solution)/shard_map/ppermute | solution.py:20
  310.5 8.4 %copy-start.5 = (bf16[4,256,4,64]{1,3,2,0:T(8,128)(2,1)S(1)}, bf16[4,256,4,64]{1,3,2,0:T(8,128)(2,1)}, u32[]{:S(2)}) copy-start(bf16[4,256,4,64]{1,3,2,0:T(8,128)(2,1)} %custom-call.7) | copy-start | bytes 1572868
  318.9 63.7 %copy-start.4 = (bf16[1,256,1024]{2,1,0:T(8,128)(2,1)S(1)}, bf16[1,256,1024]{2,1,0:T(8,128)(2,1)}, u32[]{:S(2)}) copy-start(bf16[1,256,1024]{2,1,0:T(8,128)(2,1)} %param.7) | copy-start | bytes 1572868
